TPU v7x, 32 devices: a whole 2x2x4 slice. The times are simulated.
32 devices in a mesh: grp: 1, seq: 8 (over y, x, core), ep: 4 (over z).
Axes of the slice: x: 2, y: 2, z: 4, core: 2. Of those that a mesh axis runs over, the one named last changes fastest.
Arguments:
- queries: bfloat16 [256, 64, 128], P(('grp', 'seq', 'ep')), may hold values from -110 to 110
- key_codes: bfloat16 [4352, 4, 128], P(('grp', 'seq')), may hold values from -4.5 to 4.5
- quantized_value_cache: bfloat16 [4352, 4, 128], P(('grp', 'seq')), may hold values from -4.5 to 4.5
- key_scale: bfloat16 [4352, 4], P(('grp', 'seq')), may hold values from 0.3 to 3
- value_code_scale: bfloat16 [4352, 4], P(('grp', 'seq')), may hold values from 0.29882812 to 3
- out_weight: bfloat16 [8192, 4096], P('seq', 'ep'), may hold values from -0.0625 to 0.0625
- residual: bfloat16 [256, 4096], P(('grp', 'seq', 'ep')), may hold values from -2.5 to 2.5
- norm_gain: float32 [4096], replicated, may hold values from 0.1 to 1.9
- route_ids: int32 [256, 8], P(('grp', 'seq', 'ep')), may hold values from 0 to 15, all different within a row; in each aligned block of 8 rows (0 to 7, 8 to 15, ...) at most 8 rows name the same one
- route_weight: float32 [256, 8], P(('grp', 'seq', 'ep')), may hold values from 0.1 to 1
- w_gate: bfloat16 [4096, 12288], P(None, ('seq', 'ep')), may hold values from -0.09375 to 0.09375
- w_up: bfloat16 [4096, 12288], P(None, ('seq', 'ep')), may hold values from -0.09375 to 0.09375
- w_down: bfloat16 [12288, 4096], P(('seq', 'ep')), may hold values from -0.21875 to 0.21875
Outputs:
- hidden_state: bfloat16 [256, 4096], P(('grp', 'seq', 'ep'))
- expert_out: bfloat16 [256, 4096], P(('grp', 'seq', 'ep'))
Inputs may be any that keep to these rules, and one draw needn't show every extreme that they name: `route_ids`: each token names 8 different experts; in the 8 tokens of one device (aligned blocks) no expert is named by more than 8 routes.
All inputs are finite; a program needn't handle non-finite values.
Results may differ from a plain program's by a relative error of at most 0.025.
Values may be sent and summed in bfloat16 or wider, within the bound.
A program may use at most 64 MiB of HBM per device.

v0:
```python
import math

import jax
import jax.numpy as jnp
from jax import lax
from jax.sharding import PartitionSpec as P

eps_norm = 1e-06


def block_rows(row_count):
    block_len = 1024
    while block_len > 1 and row_count % block_len != 0:
        block_len = block_len // 2
    return block_len


def key_positions(row_count, piece_len, local_len, seq_count):
    whole_idx = jnp.arange(row_count, dtype=jnp.int32)
    replica = whole_idx // (seq_count * piece_len)
    within = whole_idx % (seq_count * piece_len)
    source = within // piece_len
    offset = within % piece_len
    return source * local_len + replica * piece_len + offset


def attend(carried, pieces, positions, query_flat, query_pos, inverse):
    codes_k, codes_v, scale_k, scale_v = pieces
    row_count = codes_k.shape[0]
    block_len = block_rows(row_count)
    blocks = row_count // block_len
    head_dim = codes_k.shape[1]
    stacked = (
        codes_k.reshape(blocks, block_len, head_dim),
        codes_v.reshape(blocks, block_len, head_dim),
        scale_k.reshape(blocks, block_len),
        scale_v.reshape(blocks, block_len),
        positions.reshape(blocks, block_len),
    )

    def advance(running, block_part):
        block_k, block_v, block_ks, block_vs, block_pos = block_part
        running_max, running_sum, running_acc = running
        scores = jnp.einsum("qd,kd->qk", query_flat, block_k, preferred_element_type=jnp.float32)
        scores = scores * (block_ks.astype(jnp.float32)[None, :] * inverse)
        scores = jnp.where(block_pos[None, :] <= query_pos[:, None], scores, -jnp.inf)
        new_top = jnp.maximum(running_max, jnp.max(scores, axis=1, keepdims=True))
        safe_top = jnp.where(new_top == -jnp.inf, 0.0, new_top)
        exp_scores = jnp.exp(scores - safe_top)
        rescale = jnp.exp(running_max - safe_top)
        running_sum = running_sum * rescale + jnp.sum(exp_scores, axis=1, keepdims=True)
        weighted = (exp_scores * block_vs.astype(jnp.float32)[None, :]).astype(jnp.bfloat16)
        running_acc = running_acc * rescale + jnp.dot(
            weighted, block_v, preferred_element_type=jnp.float32
        )
        return ((new_top, running_sum, running_acc), None)

    result, unused = lax.scan(advance, carried, stacked)
    return result


def body(
    queries,
    key_codes,
    quantized_value_cache,
    key_scale,
    value_code_scale,
    out_weight,
    residual,
    norm_gain,
    route_ids,
    route_weight,
    w_gate,
    w_up,
    w_down,
):
    seq_count = lax.axis_size("seq")
    ep_count = lax.axis_size("ep")
    replica_index = lax.axis_index("ep")
    tokens_here, heads_all, head_dim = queries.shape
    local_len, kv_heads = key_scale.shape
    window_len = tokens_here * seq_count * ep_count
    prefix_len = local_len * seq_count - window_len
    local_heads = heads_all // seq_count
    copies = seq_count // kv_heads
    outgoing_kv = (key_codes, quantized_value_cache, key_scale, value_code_scale)
    outgoing_kv = tuple((jnp.repeat(member, copies, axis=1) for member in outgoing_kv))
    regrouped = (
        lax.all_to_all(queries, "seq", split_axis=1, concat_axis=0, tiled=True),
        lax.all_to_all(outgoing_kv[0], "seq", split_axis=1, concat_axis=0, tiled=True),
        lax.all_to_all(outgoing_kv[1], "seq", split_axis=1, concat_axis=0, tiled=True),
        lax.all_to_all(outgoing_kv[2], "seq", split_axis=1, concat_axis=0, tiled=True),
        lax.all_to_all(outgoing_kv[3], "seq", split_axis=1, concat_axis=0, tiled=True),
    )
    query_rows = regrouped[0]
    query_count = query_rows.shape[0]
    query_flat = query_rows.reshape(query_count * local_heads, head_dim)
    row_ids = jnp.arange(query_count, dtype=jnp.int32)
    token_pos = (
        prefix_len
        + (row_ids // tokens_here * ep_count + replica_index) * tokens_here
        + row_ids % tokens_here
    )
    query_pos = jnp.repeat(token_pos, local_heads)
    cache_part = (
        regrouped[1][:, 0, :],
        regrouped[2][:, 0, :],
        regrouped[3][:, 0],
        regrouped[4][:, 0],
    )
    inverse = 1.0 / math.sqrt(head_dim)
    flat_rows = query_count * local_heads
    initial = (
        jnp.full((flat_rows, 1), -jnp.inf, jnp.float32),
        jnp.zeros((flat_rows, 1), jnp.float32),
        jnp.zeros((flat_rows, head_dim), jnp.float32),
    )
    positions = key_positions(local_len * seq_count, local_len, local_len, seq_count)
    folded = attend(initial, cache_part, positions, query_flat, query_pos, inverse)
    running_max, running_sum, running_acc = folded
    attention = (
        (running_acc / running_sum)
        .astype(jnp.bfloat16)
        .reshape(query_count, local_heads * head_dim)
    )
    full_weight = lax.all_gather(out_weight, "ep", axis=1, tiled=True)
    picked = attention
    projected = lax.psum_scatter(
        jnp.dot(picked, full_weight, preferred_element_type=jnp.float32).astype(jnp.bfloat16),
        "seq",
        scatter_dimension=0,
        tiled=True,
    ).astype(jnp.float32)
    summed = residual.astype(jnp.float32) + projected
    hidden_state = summed.astype(jnp.bfloat16)
    hidden_wide = hidden_state.astype(jnp.float32)
    mean_square = jnp.mean(hidden_wide * hidden_wide, axis=1, keepdims=True)
    normed = (hidden_wide * lax.rsqrt(mean_square + eps_norm) * norm_gain[None, :]).astype(
        jnp.bfloat16
    )
    top_count = route_ids.shape[1]
    experts = seq_count * ep_count // 2
    capacity = max(2, min(tokens_here, 2 * tokens_here * top_count // experts))
    model_dim = residual.shape[1]
    flat_ids = route_ids.reshape(tokens_here * top_count)
    expert_grid = jnp.arange(experts, dtype=jnp.int32)
    onehot = (flat_ids[:, None] == expert_grid[None, :]).astype(jnp.int32)
    earlier = jnp.cumsum(onehot, axis=0) - onehot
    slot_index = jnp.sum(earlier * onehot, axis=1)
    expected_output = flat_ids * capacity + slot_index
    slot_grid = jnp.arange(experts * capacity, dtype=jnp.int32)
    chooser = jnp.sum(
        (
            expected_output.reshape(tokens_here, top_count)[None, :, :] == slot_grid[:, None, None]
        ).astype(jnp.bfloat16),
        axis=2,
    )
    buffer = jnp.dot(chooser, normed, preferred_element_type=jnp.float32).astype(jnp.bfloat16)
    outgoing = jnp.repeat(buffer.reshape(experts, capacity, model_dim), 2, axis=0)
    rows_in = lax.all_to_all(outgoing, ("seq", "ep"), split_axis=0, concat_axis=0, tiled=True)
    lead_count, item_count, row_width = rows_in.shape
    stacked_rows = rows_in.reshape(lead_count * item_count, row_width)
    gate_val = jnp.dot(stacked_rows, w_gate, preferred_element_type=jnp.float32)
    up_val = jnp.dot(stacked_rows, w_up, preferred_element_type=jnp.float32)
    active = (jax.nn.silu(gate_val) * up_val).astype(jnp.bfloat16)
    output = jnp.dot(active, w_down, preferred_element_type=jnp.float32).astype(jnp.bfloat16)
    answer = output.reshape(lead_count, item_count, row_width)
    returned = lax.all_to_all(answer, ("seq", "ep"), split_axis=0, concat_axis=0, tiled=True)
    pair_view = returned.reshape(experts, 2, capacity, model_dim).astype(jnp.float32)
    answers = (
        (pair_view[:, 0] + pair_view[:, 1])
        .astype(jnp.bfloat16)
        .reshape(experts * capacity, model_dim)
    )
    picked = answers[expected_output].reshape(tokens_here, top_count, model_dim)
    mix_weight = route_weight / jnp.sum(route_weight, axis=1, keepdims=True)
    expert_out = jnp.sum(mix_weight[:, :, None] * picked.astype(jnp.float32), axis=1).astype(
        jnp.bfloat16
    )
    return (hidden_state, expert_out)


def solution(mesh):
    placed = (
        P(("grp", "seq", "ep"), None, None),
        P(("grp", "seq"), None, None),
        P(("grp", "seq"), None, None),
        P(("grp", "seq"), None),
        P(("grp", "seq"), None),
        P("seq", "ep"),
        P(("grp", "seq", "ep"), None),
        P(),
        P(("grp", "seq", "ep"), None),
        P(("grp", "seq", "ep"), None),
        P(None, ("seq", "ep")),
        P(None, ("seq", "ep")),
        P(("seq", "ep"), None),
    )
    return jax.shard_map(
        body,
        mesh=mesh,
        in_specs=placed,
        out_specs=(P(("grp", "seq", "ep"), None), P(("grp", "seq", "ep"), None)),
        check_vma=False,
    )
```

profile of v0, /device:TPU:0, one launch (start us, length us, event | category | flops | bytes accessed | tf_op | source)
XLA Modules:
  0.0 389.1 jit_solution(17302106574774868218)
XLA Ops:
  10.0 5.2 %all-to-all-start.2 = ((bf16[8,2,272]{2,1,0:T(2,128)(2,1)}), bf16[8,2,272]{2,1,0:T(2,128)(2,1)S(1)}, u32[]{:S(2)}, u32[]{:S(2)}) async-start(bf16[8,2,272]{2,1,0:T(2,128)(2,1)} %reshape.130), calls=%async_computation.2 | async-start | bytes 24576 | tf_op jit(solution)/shard_map/all_to_all | solution.py:92
  17.3 2.6 all-to-all-done.2
  19.9 3.3 all-to-all-start.3
  23.2 1.6 copy.40
  24.9 3.0 all-to-all-done.3
  27.9 3.4 all-to-all-start.1
  31.3 1.9 copy.44
  33.2 3.5 all-to-all-done.1
  36.7 2.2 broadcast_in_dim.54
  38.9 4.3 %all-to-all-start.4 = ((bf16[544,8,128]{2,0,1:T(8,128)(2,1)}), bf16[544,8,128]{2,0,1:T(8,128)(2,1)}, u32[]{:S(2)}, u32[]{:S(2)}) async-start(bf16[544,8,128]{2,0,1:T(8,128)(2,1)} %bitcast.122), calls=%async_computation.4 | async-start | bytes 2228224 | tf_op jit(solution)/shard_map/all_to_all | solution.py:91
  43.2 1.9 copy.39
  45.1 14.2 %all-to-all-done.4 = bf16[544,8,128]{2,0,1:T(8,128)(2,1)} async-done(((bf16[544,8,128]{2,0,1:T(8,128)(2,1)}), bf16[544,8,128]{2,0,1:T(8,128)(2,1)}, u32[]{:S(2)}, u32[]{:S(2)}) %all-to-all-start.4) | async-done | bytes 1114144 | tf_op jit(solution)/shard_map/all_to_all | solution.py:91
  59.3 2.2 broadcast_in_dim.51
  61.5 4.3 %all-to-all-start = ((bf16[544,8,128]{2,0,1:T(8,128)(2,1)}), bf16[544,8,128]{2,0,1:T(8,128)(2,1)}, u32[]{:S(2)}, u32[]{:S(2)}) async-start(bf16[544,8,128]{2,0,1:T(8,128)(2,1)} %bitcast.121), calls=%async_computation | async-start | bytes 2228224 | tf_op jit(solution)/shard_map/all_to_all | solution.py:90
  76.3 5.6 %all-to-all-done = bf16[544,8,128]{2,0,1:T(8,128)(2,1)} async-done(((bf16[544,8,128]{2,0,1:T(8,128)(2,1)}), bf16[544,8,128]{2,0,1:T(8,128)(2,1)}, u32[]{:S(2)}, u32[]{:S(2)}) %all-to-all-start) | async-done | bytes 1114144 | tf_op jit(solution)/shard_map/all_to_all | solution.py:90
  81.9 117.2 %while.15 = (s32[]{:T(128)}, f32[512,1]{0,1:T(1,128)S(1)}, f32[512,1]{0,1:T(1,128)S(1)}, f32[512,128]{1,0:T(8,128)S(1)}, s32[17,256]{1,0:T(8,128)}, /*index=5*/b...) while((s32[]{:T(128)}, f32[512,1]{0,1:T(1,128)S(1)}, ...), condition=%wide.region_3.4_spmd.clone, body=%wide.region_0.3_spmd.clone.sunk | while | flops 68490496 | bytes 2411925 | solution.py:58
  83.5 2.0 fusion.93
  90.4 2.0 fusion.93
  97.3 2.0 fusion.93
  101.1 1.4 convolution_add_fusion.2
  104.2 2.0 fusion.93
  111.1 2.0 fusion.93
  118.0 2.0 fusion.93
  124.8 2.0 fusion.93
  131.7 2.0 fusion.93
  135.6 1.4 convolution_add_fusion.2
  138.6 2.0 fusion.93
  142.5 1.4 convolution_add_fusion.2
  145.5 2.0 fusion.93
  152.4 2.0 fusion.93
  156.3 1.4 convolution_add_fusion.2
  159.3 2.0 fusion.93
  166.2 2.0 fusion.93
  173.1 2.0 fusion.93
  180.0 2.0 fusion.93
  186.9 2.0 fusion.93
  193.8 2.0 fusion.93
  199.4 20.1 %all-gather.2.cloned.1.call-done = bf16[1024,4096]{1,0:T(8,128)(2,1)} async-done(((bf16[1024,1024]{1,0:T(8,128)(2,1)}), bf16[1024,4096]{1,0:T(8,128)(2,1)}) %all-gather.2.cloned.1.call-update) | async-done | bytes 8388624 | tf_op jit(solution)/shard_map/all_gather | solution.py:126
  219.5 5.8 %convolution_convert_fusion.2 = bf16[64,4096]{1,0:T(8,128)(2,1)} fusion(bf16[64,1024]{1,0:T(8,128)(2,1)S(1)} %reshape.111, bf16[1024,4096]{1,0:T(8,128)(2,1)} %all-gather.2.cloned.1.call-done), kind=kOutput, calls=%fused_computation.35 | convolution fusion | flops 537133056 | bytes 9043968 | tf_op jit(solution)/shard_map/dot_general | solution.py:129
  225.9 31.9 %reduce-scatter.2.cloned.1.call-done = bf16[8,4096]{1,0:T(8,128)(2,1)} async-done(((bf16[64,4096]{1,0:T(8,128)(2,1)}), bf16[8,4096]{1,0:T(8,128)(2,1)}) %reduce-scatter.2.cloned.1.call-update) | async-done | bytes 65552 | tf_op jit(solution)/shard_map/reduce_scatter | solution.py:128
  259.6 51.9 %all_to_all.89 = bf16[32,8,4096]{2,1,0:T(8,128)(2,1)S(1)} all-to-all(bf16[32,8,4096]{2,1,0:T(8,128)(2,1)S(1)} %bitcast.120), channel_id=1, replica_groups=mesh['grp'=1,'seq'=8,'ep'=4] {'seq','ep'}, dimensions={0} | all-to-all | bytes 4194304 | tf_op jit(solution)/shard_map/all_to_all | solution.py:160
  312.8 2.1 fusion.25
  314.9 6.4 %fusion.19 = bf16[32,8,4096]{2,1,0:T(8,128)(2,1)} fusion(bf16[384,4096]{1,0:T(8,128)(2,1)S(1)} %copy-done, bf16[4096,384]{1,0:T(8,128)(2,1)} %param.26, bf16[32,8,4096]{2,1,0:T(8,128)(2,1)} %copy-done.1, f32[256,384]{1,0:T(8,128)} %fusion.25), kind=kOutput, calls=%fused_computation.32 | convolution fusion | flops 1612251136 | bytes 10878976 | tf_op jit(solution)/shard_map/dot_general | solution.py:166
  321.3 4.6 %all-to-all-start.6 = ((bf16[32,8,4096]{2,1,0:T(8,128)(2,1)}), bf16[32,8,4096]{2,1,0:T(8,128)(2,1)}, u32[]{:S(2)}, u32[]{:S(2)}) async-start(bf16[32,8,4096]{2,1,0:T(8,128)(2,1)} %fusion.19), calls=%async_computation.7 | async-start | bytes 4194304 | tf_op jit(solution)/shard_map/all_to_all | solution.py:168
  326.2 47.2 %all-to-all-done.6 = bf16[32,8,4096]{2,1,0:T(8,128)(2,1)} async-done(((bf16[32,8,4096]{2,1,0:T(8,128)(2,1)}), bf16[32,8,4096]{2,1,0:T(8,128)(2,1)}, u32[]{:S(2)}, u32[]{:S(2)}) %all-to-all-start.6) | async-done | bytes 2097184 | tf_op jit(solution)/shard_map/all_to_all | solution.py:168
  373.4 2.1 convert.4
  376.6 3.5 gather_fusion
  380.2 2.1 fusion.34
  (230 shorter events, 97.4 us)
Async XLA Ops:
  7.2 307.7 %copy-start = (bf16[384,4096]{1,0:T(8,128)(2,1)S(1)}, bf16[384,4096]{1,0:T(8,128)(2,1)}, u32[]{:S(2)}) copy-start(bf16[384,4096]{1,0:T(8,128)(2,1)} %param.27) | copy-start | bytes 9437188
  10.0 9.9 %all-to-all-start.2 = ((bf16[8,2,272]{2,1,0:T(2,128)(2,1)}), bf16[8,2,272]{2,1,0:T(2,128)(2,1)S(1)}, u32[]{:S(2)}, u32[]{:S(2)}) async-start(bf16[8,2,272]{2,1,0:T(2,128)(2,1)} %reshape.130), calls=%async_computation.2 | async-start | bytes 24576 | tf_op jit(solution)/shard_map/all_to_all | solution.py:92
  19.9 19.0 %copy-start.4 = (bf16[8,2,272]{2,1,0:T(2,128)(2,1)}, bf16[8,2,272]{2,1,0:T(2,128)(2,1)S(1)}, u32[]{:S(2)}) copy-start(bf16[8,2,272]{2,1,0:T(2,128)(2,1)S(1)} %all-to-all-done.2) | copy-start | bytes 26116
  19.9 8.0 %all-to-all-start.3 = ((bf16[8,2,272]{2,1,0:T(2,128)(2,1)}), bf16[8,2,272]{2,1,0:T(2,128)(2,1)S(1)}, u32[]{:S(2)}, u32[]{:S(2)}) async-start(bf16[8,2,272]{2,1,0:T(2,128)(2,1)} %reshape.132), calls=%async_computation.3 | async-start | bytes 24576 | tf_op jit(solution)/shard_map/all_to_all | solution.py:93
  27.9 11.0 %copy-start.5 = (bf16[8,2,272]{2,1,0:T(2,128)(2,1)}, bf16[8,2,272]{2,1,0:T(2,128)(2,1)S(1)}, u32[]{:S(2)}) copy-start(bf16[8,2,272]{2,1,0:T(2,128)(2,1)S(1)} %all-to-all-done.3) | copy-start | bytes 26116
  27.9 8.8 %all-to-all-start.1 = ((bf16[8,64,128]{2,0,1:T(8,128)(2,1)}), bf16[8,64,128]{2,0,1:T(8,128)(2,1)S(1)}, u32[]{:S(2)}, u32[]{:S(2)}) async-start(bf16[8,64,128]{2,0,1:T(8,128)(2,1)} %copy.40), calls=%async_computation.1 | async-start | bytes 262144 | tf_op jit(solution)/shard_map/all_to_all | solution.py:89
  38.9 20.4 %all-to-all-start.4 = ((bf16[544,8,128]{2,0,1:T(8,128)(2,1)}), bf16[544,8,128]{2,0,1:T(8,128)(2,1)}, u32[]{:S(2)}, u32[]{:S(2)}) async-start(bf16[544,8,128]{2,0,1:T(8,128)(2,1)} %bitcast.122), calls=%async_computation.4 | async-start | bytes 2228224 | tf_op jit(solution)/shard_map/all_to_all | solution.py:91
  61.5 20.4 %all-to-all-start = ((bf16[544,8,128]{2,0,1:T(8,128)(2,1)}), bf16[544,8,128]{2,0,1:T(8,128)(2,1)}, u32[]{:S(2)}, u32[]{:S(2)}) async-start(bf16[544,8,128]{2,0,1:T(8,128)(2,1)} %bitcast.121), calls=%async_computation | async-start | bytes 2228224 | tf_op jit(solution)/shard_map/all_to_all | solution.py:90
  65.8 153.7 %all-gather.2.cloned.1.call-start = ((), (), s32[]{:S(2)}) async-start(), calls=%async_computation.8 | async-start | bytes 10485760 | tf_op jit(solution)/shard_map/all_gather | solution.py:126
  66.5 191.3 %reduce-scatter.2.cloned.1.call-start = ((), (), s32[]{:S(2)}) async-start(), calls=%async_computation.9 | async-start | bytes 589824 | tf_op jit(solution)/shard_map/reduce_scatter | solution.py:128
  199.4 25.9 %copy-start.8 = (s32[8,8]{1,0:T(8,128)S(1)}, s32[8,8]{1,0:T(8,128)}, u32[]{:S(2)}) copy-start(s32[8,8]{1,0:T(8,128)} %param.23) | copy-start | bytes 772
  199.4 58.4 %copy-start.3 = (bf16[8,4096]{1,0:T(8,128)(2,1)S(1)}, bf16[8,4096]{1,0:T(8,128)(2,1)}, u32[]{:S(2)}) copy-start(bf16[8,4096]{1,0:T(8,128)(2,1)} %param.21) | copy-start | bytes 196612
  199.4 59.4 %copy-start.6 = (f32[4096]{0:T(1024)S(1)}, f32[4096]{0:T(1024)}, u32[]{:S(2)}) copy-start(f32[4096]{0:T(1024)} %param.22) | copy-start | bytes 49156
  258.8 0.8 copy-start.2
  259.6 53.2 %copy-start.9 = (bf16[4096,384]{1,0:T(8,128)(2,1)S(1)}, bf16[4096,384]{1,0:T(8,128)(2,1)}, u32[]{:S(2)}) copy-start(bf16[4096,384]{1,0:T(8,128)(2,1)} %param.25) | copy-start | bytes 9437188
  311.5 1.3 copy-start.1
  321.3 4.7 %copy-start.7 = (f32[8,8]{1,0:T(8,128)S(1)}, f32[8,8]{1,0:T(8,128)}, u32[]{:S(2)}) copy-start(f32[8,8]{1,0:T(8,128)} %param.24) | copy-start | bytes 772
  321.3 52.1 %all-to-all-start.6 = ((bf16[32,8,4096]{2,1,0:T(8,128)(2,1)}), bf16[32,8,4096]{2,1,0:T(8,128)(2,1)}, u32[]{:S(2)}, u32[]{:S(2)}) async-start(bf16[32,8,4096]{2,1,0:T(8,128)(2,1)} %fusion.19), calls=%async_computation.7 | async-start | bytes 4194304 | tf_op jit(solution)/shard_map/all_to_all | solution.py:168
Sparse Core Ops, SparseCore 0:
  68.2 151.2 all-gather.1
  225.4 32.3 reduce-scatter.1
where the time goes:
time: 394 us; the launch traced here: 389 us
  waiting for transfers between devices  129 us (33%)
  matrix products  73.1 us (19%)
  other arithmetic  52.9 us (13%)
  blocking collectives  51.9 us (13%)
  local copies, waits for them, and re-layouts  42.5 us (11%)
  starting transfers between devices  25.1 us (6%)
  between operations  14.3 us (4%)
    all_to_all x1, blocking collectives, body(): lax.all_to_all(outgoing, ('seq', 'ep'), split_axis=0, concat_axis=0, tile...  51.9 us
    all_to_all x1, waiting for transfers between devices, body(): lax.all_to_all(answer, ('seq', 'ep'), split_axis=0, concat_axis=0, tiled=...  47.2 us
    dot_general x17, matrix products, advance(): jnp.einsum('qd,kd->qk', query_flat, block_k, preferred_element_type=jnp.f...  34.3 us
    reduce_scatter x1, waiting for transfers between devices, body(): lax.psum_scatter(jnp.dot(picked, full_weight, preferred_element_type=jnp....  31.9 us
    dot_general x17, matrix products, advance(): jnp.dot(weighted, block_v, preferred_element_type=jnp.float32)  24 us
    all_gather x1, waiting for transfers between devices, body(): full_weight = lax.all_gather(out_weight, 'ep', axis=1, tiled=True)  20.1 us
    reduce_sum x17, other arithmetic, advance(): jnp.sum(exp_scores, axis=1, keepdims=True)  19.5 us
    all_to_all x1, waiting for transfers between devices, body(): lax.all_to_all(outgoing_kv[1], 'seq', split_axis=1, concat_axis=0, tiled=...  14.2 us
  transfers between devices with their start and end apart: 8, of which 8 were waited for; matrix products, arithmetic and copies ran while one was open for 35% of the time, Pallas kernels for 0%

commit v1 on v0

v1 whole, which is shorter than its diff:
```python
import functools
import math

import jax
import jax.numpy as jnp
from jax import lax
from jax.experimental import pallas as pl
from jax.experimental.pallas import tpu as pltpu
from jax.sharding import PartitionSpec as P

eps_norm = 1e-06
MESH = pl.DeviceIdType.MESH
hidden_score = -1e30


def device_at(seq_pos, ep_pos):
    return {"seq": seq_pos, "ep": ep_pos}


def remote(src, dst, send_sem, recv_sem, seq_pos, ep_pos):
    return pltpu.make_async_remote_copy(
        src_ref=src,
        dst_ref=dst,
        send_sem=send_sem,
        recv_sem=recv_sem,
        device_id=device_at(seq_pos, ep_pos),
        device_id_type=MESH,
    )


def attention_kernel(
    n_seq,
    n_ep,
    copies,
    tokens,
    heads,
    prefix_len,
    q_ref,
    kv_ref,
    scale_ref,
    out_ref,
    q_all,
    kv_all,
    scale_all,
    top,
    total,
    acc,
    wide,
    q_send,
    q_recv,
    kv_send,
    kv_recv,
    scale_send,
    scale_recv,
    own_sem,
):
    me = lax.axis_index("seq")
    zed = lax.axis_index("ep")
    groups = n_seq // copies
    group = me // copies
    member = me % copies
    head_dim = q_ref.shape[2]
    local_len = scale_ref.shape[2]
    rows_each = tokens * heads

    barrier = pltpu.get_barrier_semaphore()
    for step in range(1, n_seq):
        pl.semaphore_signal(
            barrier,
            inc=1,
            device_id=device_at((me + step) % n_seq, zed),
            device_id_type=MESH,
        )
    own = pltpu.make_async_copy(q_ref.at[me], q_all.at[me], own_sem)
    own.start()
    top[...] = jnp.full_like(top, hidden_score)
    total[...] = jnp.zeros_like(total)
    acc[...] = jnp.zeros_like(acc)
    pl.semaphore_wait(barrier, n_seq - 1)

    pending = []
    q_copies = []
    for step in range(1, n_seq):
        to = (me + step) % n_seq
        c = remote(q_ref.at[to], q_all.at[me], q_send.at[step], q_recv.at[step], to, zed)
        c.start()
        q_copies.append(c)

    def send_kv(kv_src, scale_src, i, q, to):
        a = remote(kv_src, kv_all.at[i, q], kv_send.at[i, q], kv_recv.at[i, q], to, zed)
        b = remote(
            scale_src, scale_all.at[i, q], scale_send.at[i, q], scale_recv.at[i, q], to, zed
        )
        a.start()
        b.start()
        pending.append((a, b))
        return (a, b)

    arrivals = {}
    for i in range(1, groups):
        goal = (group + i) % groups
        arrivals[i, 0] = send_kv(
            kv_ref.at[goal], scale_ref.at[goal], i, 0, goal * copies + member
        )
    for q in range(1, copies):
        arrivals[0, q] = send_kv(
            kv_ref.at[group],
            scale_ref.at[group],
            0,
            q,
            group * copies + (member + q) % copies,
        )

    own.wait()
    for c in q_copies:
        c.wait_recv()

    row_tile = 128
    row_tiles = n_seq * rows_each // row_tile
    inverse = 1.0 / math.sqrt(head_dim)

    def attend(kv, scales, i, q):
        source = ((group + groups - i) % groups) * copies + (member + copies - q) % copies

        def one_tile(n, unused):
            at = pl.ds(pl.multiple_of(n * row_tile, row_tile), row_tile)
            queries = q_all[pl.ds(n * (row_tile // rows_each), row_tile // rows_each)].reshape(
                row_tile, head_dim
            )
            keys = kv[pl.ds(0, local_len), :]
            scores = lax.dot_general(
                queries, keys, (((1,), (1,)), ((), ())), preferred_element_type=jnp.float32
            )
            scores = scores * (scales[0:1, :] * inverse)
            key_pos = source * local_len + lax.broadcasted_iota(jnp.int32, (1, local_len), 1)
            row = n * row_tile + lax.broadcasted_iota(jnp.int32, (row_tile, 1), 0)
            query_pos = prefix_len + ((row // rows_each) * n_ep + zed) * tokens + row % tokens
            scores = jnp.where(key_pos <= query_pos, scores, hidden_score)
            old = top[at, :]
            new = jnp.maximum(old, jnp.max(scores, axis=1, keepdims=True))
            exp_scores = jnp.exp(scores - new[:, :1])
            shrink = jnp.exp(old - new)
            total[at, :] = total[at, :] * shrink + jnp.sum(exp_scores, axis=1, keepdims=True)
            weighted = (exp_scores * scales[1:2, :]).astype(jnp.bfloat16)
            acc[at, :] = acc[at, :] * shrink + jnp.dot(
                weighted, kv[pl.ds(local_len, local_len), :], preferred_element_type=jnp.float32
            )
            top[at, :] = new
            return unused

        lax.fori_loop(0, row_tiles, one_tile, 0)

    attend(kv_ref.at[group], scale_ref.at[group], 0, 0)
    for q in range(1, copies):
        for c in arrivals[0, q]:
            c.wait_recv()
        attend(kv_all.at[0, q], scale_all.at[0, q], 0, q)
    for i in range(1, groups):
        for c in arrivals[i, 0]:
            c.wait_recv()
        for q in range(1, copies):
            arrivals[i, q] = send_kv(
                kv_all.at[i, 0],
                scale_all.at[i, 0],
                i,
                q,
                group * copies + (member + q) % copies,
            )
        attend(kv_all.at[i, 0], scale_all.at[i, 0], i, 0)
    for i in range(1, groups):
        for q in range(1, copies):
            for c in arrivals[i, q]:
                c.wait_recv()
            attend(kv_all.at[i, q], scale_all.at[i, q], i, q)

    for src in range(n_seq):
        for h in range(heads):
            at = pl.ds(src * rows_each + h * tokens, tokens)
            wide[pl.ds(src * tokens, tokens), pl.ds(h * head_dim, head_dim)] = (
                acc[at, :] / total[at, :]
            )
    out_ref[...] = wide[...].astype(jnp.bfloat16)
    for c in q_copies:
        c.wait_send()
    for pair in pending:
        for c in pair:
            c.wait_send()


def layer_kernel(
    n_seq,
    n_ep,
    tokens,
    attn_ref,
    out_weight_ref,
    residual_ref,
    gain_ref,
    mix_ref,
    gate_ref,
    up_ref,
    down_ref,
    hidden_ref,
    expert_ref,
    attn_all,
    out_w,
    gate_w,
    up_w,
    down_w,
    part_out,
    part_in,
    col_out,
    col_in,
    mine,
    gathered,
    rows,
    gate_acc,
    up_acc,
    active,
    partial,
    pair_in,
    pair_sum,
    plane_in,
    tail_own,
    tail_out,
    tail_in,
    load_sem,
    local_sem,
    attn_send,
    attn_recv,
    part_send,
    part_recv,
    col_send,
    col_recv,
    a_send,
    a_recv,
    b_send,
    b_recv,
    c_send,
    c_recv,
    pair_send,
    pair_recv,
    plane_send,
    plane_recv,
    tail_send,
    tail_recv,
):
    me = lax.axis_index("seq")
    zed = lax.axis_index("ep")
    chips = n_seq // 2
    chip = me // 2
    core = me % 2
    other = chip * 2 + (1 - core)
    model = residual_ref.shape[1]
    half = model // 2
    bf16 = jnp.bfloat16
    f32 = jnp.float32

    loads = []
    for n, (src, dst) in enumerate(
        ((out_weight_ref, out_w), (gate_ref, gate_w), (up_ref, up_w), (down_ref, down_w))
    ):
        c = pltpu.make_async_copy(src, dst, load_sem.at[n])
        c.start()
        loads.append(c)

    barrier = pltpu.get_barrier_semaphore()
    for step in range(1, n_seq):
        pl.semaphore_signal(
            barrier, inc=1, device_id=device_at((me + step) % n_seq, zed), device_id_type=MESH
        )
    for step in range(1, n_ep):
        pl.semaphore_signal(
            barrier, inc=1, device_id=device_at(me, (zed + step) % n_ep), device_id_type=MESH
        )
    own = pltpu.make_async_copy(attn_ref, attn_all.at[zed], local_sem.at[0])
    own.start()
    pl.semaphore_wait(barrier, n_seq + n_ep - 2)

    sends = []

    def go(*args):
        c = remote(*args)
        c.start()
        sends.append(c)
        return c

    waits = [
        go(
            attn_ref,
            attn_all.at[zed],
            attn_send.at[j],
            attn_recv.at[j],
            me,
            (zed + j) % n_ep,
        )
        for j in range(1, n_ep)
    ]
    own.wait()
    loads[0].wait()
    for c in waits:
        c.wait_recv()

    cols = out_w.shape[1]
    depth = attn_ref.shape[1]
    part_waits = []
    attention = attn_all[...].reshape(n_ep * n_seq * tokens, depth)
    col_tile = 256
    for n in range(cols // col_tile):
        at = pl.ds(n * col_tile, col_tile)
        product = jnp.dot(attention, out_w[:, at], preferred_element_type=f32).reshape(
            n_ep, n_seq, tokens, col_tile
        )
        for s in range(n_seq):
            part_out[s, :, at] = product[:, s].reshape(n_ep * tokens, col_tile).astype(bf16)
    for step in range(1, n_seq):
        to = (me + step) % n_seq
        part_waits.append(
            go(
                part_out.at[to],
                part_in.at[step],
                part_send.at[step],
                part_recv.at[step],
                to,
                zed,
            )
        )
    for c in part_waits:
        c.wait_recv()
    summed = part_out[me].astype(f32)
    for step in range(1, n_seq):
        summed = summed + part_in[step].astype(f32)
    col_out[...] = summed.reshape(n_ep, tokens, cols)
    col_waits = []
    for j in range(1, n_ep):
        to = (zed + j) % n_ep
        col_waits.append(
            go(col_out.at[to], col_in.at[zed], col_send.at[j], col_recv.at[j], me, to)
        )
    keep = pltpu.make_async_copy(col_out.at[zed], col_in.at[zed], local_sem.at[1])
    keep.start()
    keep.wait()
    for c in col_waits:
        c.wait_recv()
    projected = jnp.concatenate([col_in[j] for j in range(n_ep)], axis=1)
    hidden = (residual_ref[...].astype(f32) + projected).astype(bf16)
    hidden_ref[...] = hidden
    wide = hidden.astype(f32)
    mean_square = jnp.mean(wide * wide, axis=1, keepdims=True)
    normed = wide * lax.rsqrt(mean_square + eps_norm) * gain_ref[...]
    mine[...] = jnp.concatenate([normed[:, :half], normed[:, half:]], axis=0).astype(bf16)

    keep = pltpu.make_async_copy(mine, gathered.at[core, chip, zed], local_sem.at[2])
    keep.start()
    spot = gathered.at[core, chip, zed]
    a_waits = {}
    b_waits = {}
    c_waits = []
    for j in range(1, n_ep):
        a_waits[j] = go(mine, spot, a_send.at[j], a_recv.at[j], me, (zed + j) % n_ep)

    def spread(src, at, j):
        for i in range(1, chips):
            to = ((chip + i) % chips) * 2 + core
            b_waits[i, j] = go(src, at, b_send.at[i, j], b_recv.at[i, j], to, zed)

    def across(src, at, i, j):
        c_waits.append(go(src, at, c_send.at[i, j], c_recv.at[i, j], other, zed))

    spread(mine, spot, 0)
    across(mine, spot, 0, 0)
    for j in range(1, n_ep):
        a_waits[j].wait_recv()
        at = gathered.at[core, chip, (zed + n_ep - j) % n_ep]
        spread(at, at, j)
        across(at, at, 0, j)
    for j in range(n_ep):
        for i in range(1, chips):
            b_waits[i, j].wait_recv()
            at = gathered.at[core, (chip + chips - i) % chips, (zed + n_ep - j) % n_ep]
            across(at, at, i, j)
    keep.wait()
    for c in c_waits:
        c.wait_recv()

    pairs = n_ep // 2

    def regroup(n, unused):
        blocks = gathered[n // (chips * pairs), (n // pairs) % chips, pl.ds((n % pairs) * 2, 2)]
        blocks = blocks.astype(f32)
        at = pl.ds(pl.multiple_of(n * 16, 16), 16)
        rows[at, pl.ds(0, half)] = jnp.concatenate(
            [blocks[0, :tokens], blocks[1, :tokens]], axis=0
        ).astype(bf16)
        rows[at, pl.ds(half, half)] = jnp.concatenate(
            [blocks[0, tokens:], blocks[1, tokens:]], axis=0
        ).astype(bf16)
        return unused

    lax.fori_loop(0, 2 * chips * pairs, regroup, 0)

    for c in loads[1:]:
        c.wait()
    gate_acc[...] = jnp.zeros_like(gate_acc)
    up_acc[...] = jnp.zeros_like(up_acc)
    depth_tile = 1024
    row_tile = 256
    count = rows.shape[0]

    def contract(n, unused):
        deep = pl.ds(pl.multiple_of(n * depth_tile, depth_tile), depth_tile)
        for r in range(count // row_tile):
            at = pl.ds(r * row_tile, row_tile)
            part = rows[at, deep]
            gate_acc[at, :] += jnp.dot(part, gate_w[deep, :], preferred_element_type=f32)
            up_acc[at, :] += jnp.dot(part, up_w[deep, :], preferred_element_type=f32)
        return unused

    lax.fori_loop(0, model // depth_tile, contract, 0)
    gate = gate_acc[...]
    active[...] = (gate / (1.0 + jnp.exp(-gate)) * up_acc[...]).astype(bf16)

    chunks = partial.shape[0]
    width = partial.shape[2]
    my_rows = count // 2
    chip_rows = n_ep * tokens
    pair_waits, plane_waits, tail_waits = {}, {}, {}

    def down(ch):
        deep = pl.ds(ch * width, width)
        for r in range(count // row_tile):
            at = pl.ds(r * row_tile, row_tile)
            for n in range(width // 256):
                deep = pl.ds(ch * width + n * 256, 256)
                y = jnp.dot(active[at, :], down_w[:, deep], preferred_element_type=f32)
                partial[ch, at, pl.ds(n * 256, 256)] = (y * mix_ref[at, :1]).astype(bf16)
        theirs = pl.ds(pl.multiple_of((1 - core) * my_rows, 16), my_rows)
        pair_waits[ch] = go(
            partial.at[ch, theirs],
            pair_in.at[ch],
            pair_send.at[ch],
            pair_recv.at[ch],
            other,
            zed,
        )

    def over_pair(ch):
        pair_waits[ch].wait_recv()
        ours = pl.ds(pl.multiple_of(core * my_rows, 16), my_rows)
        pair_sum[ch] = (partial[ch, ours, :].astype(f32) + pair_in[ch].astype(f32)).astype(bf16)
        for i in range(1, chips):
            goal = (chip + i) % chips
            plane_waits[ch, i] = go(
                pair_sum.at[ch, pl.ds(pl.multiple_of(goal * chip_rows, 16), chip_rows)],
                plane_in.at[ch, i],
                plane_send.at[ch, i],
                plane_recv.at[ch, i],
                goal * 2 + core,
                zed,
            )

    def over_plane(ch):
        for i in range(1, chips):
            plane_waits[ch, i].wait_recv()
        ours = pl.ds(pl.multiple_of(chip * chip_rows, 16), chip_rows)
        value = pair_sum[ch, ours, :].astype(f32)
        for i in range(1, chips):
            value = value + plane_in[ch, i].astype(f32)
        tail_own[ch] = value.reshape(n_ep, tokens, width)
        for j in range(n_ep):
            block = value[j * tokens : (j + 1) * tokens]
            tail_out[ch, j] = jnp.concatenate(
                [block[:, : width // 2], block[:, width // 2 :]], axis=0
            ).astype(bf16)
        for j in range(1, n_ep):
            to = (zed + j) % n_ep
            tail_waits[ch, j] = go(
                tail_out.at[ch, to],
                tail_in.at[ch, j],
                tail_send.at[ch, j],
                tail_recv.at[ch, j],
                me,
                to,
            )

    def finish(ch):
        value = tail_own[ch, zed]
        for j in range(1, n_ep):
            tail_waits[ch, j].wait_recv()
            got = tail_in[ch, j].astype(f32)
            value = value + jnp.concatenate([got[:tokens], got[tokens:]], axis=1)
        expert_ref[:, pl.ds(ch * width, width)] = value.astype(bf16)

    for step in range(chunks + 3):
        if step < chunks:
            down(step)
        if 0 <= step - 1 < chunks:
            over_pair(step - 1)
        if 0 <= step - 2 < chunks:
            over_plane(step - 2)
        if 0 <= step - 3 < chunks:
            finish(step - 3)
    for c in sends:
        c.wait_send()


def body(
    queries,
    key_codes,
    quantized_value_cache,
    key_scale,
    value_code_scale,
    out_weight,
    residual,
    norm_gain,
    route_ids,
    route_weight,
    w_gate,
    w_up,
    w_down,
):
    n_seq = lax.axis_size("seq")
    n_ep = lax.axis_size("ep")
    tokens, heads_all, head_dim = queries.shape
    local_len, kv_heads = key_scale.shape
    window_len = tokens * n_seq * n_ep
    prefix_len = local_len * n_seq - window_len
    heads = heads_all // n_seq
    copies = n_seq // kv_heads
    groups = n_seq // copies
    bf16, f32 = jnp.bfloat16, jnp.float32
    model = residual.shape[1]
    experts = n_seq * n_ep // 2

    mix = route_weight / jnp.sum(route_weight, axis=1, keepdims=True)
    grid = jnp.arange(experts, dtype=jnp.int32)
    dense = jnp.sum(
        jnp.where(route_ids[:, :, None] == grid[None, None, :], mix[:, :, None], 0.0), axis=1
    )
    everyone = lax.all_gather(dense, ("seq", "ep"), axis=0, tiled=True)
    expert = (lax.axis_index("seq") * n_ep + lax.axis_index("ep")) // 2
    my_mix = jnp.sum(jnp.where(grid[None, :] == expert, everyone, 0.0), axis=1)
    my_mix = my_mix.reshape(n_seq // 2, 2, n_ep * tokens).transpose(1, 0, 2)
    my_mix = jnp.broadcast_to(my_mix.reshape(window_len, 1), (window_len, 128))

    q_sorted = (
        queries.reshape(tokens, n_seq, heads, head_dim)
        .transpose(1, 2, 0, 3)
        .reshape(n_seq, heads * tokens, head_dim)
    )
    kv = jnp.concatenate(
        [key_codes.transpose(1, 0, 2), quantized_value_cache.transpose(1, 0, 2)], axis=1
    )
    scales = jnp.stack([key_scale.T, value_code_scale.T], axis=1).astype(f32)
    scales = jnp.pad(scales, ((0, 0), (0, 6), (0, 0)))
    q_rows = n_seq * heads * tokens
    vmem = pl.BlockSpec(memory_space=pltpu.VMEM)
    hbm = pl.BlockSpec(memory_space=pl.ANY)
    dma = pltpu.SemaphoreType.DMA
    attention = pl.pallas_call(
        functools.partial(attention_kernel, n_seq, n_ep, copies, tokens, heads, prefix_len),
        out_shape=jax.ShapeDtypeStruct((n_seq * tokens, heads * head_dim), bf16),
        in_specs=[vmem] * 3,
        out_specs=vmem,
        scratch_shapes=[
            pltpu.VMEM((n_seq, heads * tokens, head_dim), bf16),
            pltpu.VMEM((groups, copies, 2 * local_len, head_dim), bf16),
            pltpu.VMEM((groups, copies, 8, local_len), f32),
            pltpu.VMEM((q_rows, head_dim), f32),
            pltpu.VMEM((q_rows, head_dim), f32),
            pltpu.VMEM((q_rows, head_dim), f32),
            pltpu.VMEM((n_seq * tokens, heads * head_dim), f32),
            dma((n_seq,)),
            dma((n_seq,)),
            dma((groups, copies)),
            dma((groups, copies)),
            dma((groups, copies)),
            dma((groups, copies)),
            dma,
        ],
        compiler_params=pltpu.CompilerParams(
            collective_id=0, has_side_effects=True, vmem_limit_bytes=40 << 20
        ),
        name="attention",
    )(q_sorted, kv, scales)

    cols = out_weight.shape[1]
    depth = out_weight.shape[0]
    wide = w_gate.shape[1]
    chips = n_seq // 2
    chunks = 4
    width = model // chunks
    return pl.pallas_call(
        functools.partial(layer_kernel, n_seq, n_ep, tokens),
        out_shape=(
            jax.ShapeDtypeStruct((tokens, model), bf16),
            jax.ShapeDtypeStruct((tokens, model), bf16),
        ),
        in_specs=[vmem, hbm, vmem, vmem, vmem, hbm, hbm, hbm],
        out_specs=(vmem, vmem),
        scratch_shapes=[
            pltpu.VMEM((n_ep, n_seq * tokens, depth), bf16),
            pltpu.VMEM((depth, cols), bf16),
            pltpu.VMEM((model, wide), bf16),
            pltpu.VMEM((model, wide), bf16),
            pltpu.VMEM((wide, model), bf16),
            pltpu.VMEM((n_seq, n_ep * tokens, cols), bf16),
            pltpu.VMEM((n_seq, n_ep * tokens, cols), bf16),
            pltpu.VMEM((n_ep, tokens, cols), f32),
            pltpu.VMEM((n_ep, tokens, cols), f32),
            pltpu.VMEM((2 * tokens, model // 2), bf16),
            pltpu.VMEM((2, chips, n_ep, 2 * tokens, model // 2), bf16),
            pltpu.VMEM((window_len, model), bf16),
            pltpu.VMEM((window_len, wide), f32),
            pltpu.VMEM((window_len, wide), f32),
            pltpu.VMEM((window_len, wide), bf16),
            pltpu.VMEM((chunks, window_len, width), bf16),
            pltpu.VMEM((chunks, window_len // 2, width), bf16),
            pltpu.VMEM((chunks, window_len // 2, width), bf16),
            pltpu.VMEM((chunks, chips, n_ep * tokens, width), bf16),
            pltpu.VMEM((chunks, n_ep, tokens, width), f32),
            pltpu.VMEM((chunks, n_ep, 2 * tokens, width // 2), bf16),
            pltpu.VMEM((chunks, n_ep, 2 * tokens, width // 2), bf16),
            dma((4,)),
            dma((3,)),
            dma((n_ep,)),
            dma((n_ep,)),
            dma((n_seq,)),
            dma((n_seq,)),
            dma((n_ep,)),
            dma((n_ep,)),
            dma((n_ep,)),
            dma((n_ep,)),
            dma((chips, n_ep)),
            dma((chips, n_ep)),
            dma((chips, n_ep)),
            dma((chips, n_ep)),
            dma((chunks,)),
            dma((chunks,)),
            dma((chunks, chips)),
            dma((chunks, chips)),
            dma((chunks, n_ep)),
            dma((chunks, n_ep)),
        ],
        compiler_params=pltpu.CompilerParams(
            collective_id=1, has_side_effects=True, vmem_limit_bytes=60 << 20
        ),
        name="layer",
    )(
        attention,
        out_weight,
        residual,
        norm_gain.reshape(1, model),
        my_mix,
        w_gate,
        w_up,
        w_down,
    )


def solution(mesh):
    placed = (
        P(("grp", "seq", "ep"), None, None),
        P(("grp", "seq"), None, None),
        P(("grp", "seq"), None, None),
        P(("grp", "seq"), None),
        P(("grp", "seq"), None),
        P("seq", "ep"),
        P(("grp", "seq", "ep"), None),
        P(),
        P(("grp", "seq", "ep"), None),
        P(("grp", "seq", "ep"), None),
        P(None, ("seq", "ep")),
        P(None, ("seq", "ep")),
        P(("seq", "ep"), None),
    )
    return jax.shard_map(
        body,
        mesh=mesh,
        in_specs=placed,
        out_specs=(P(("grp", "seq", "ep"), None), P(("grp", "seq", "ep"), None)),
        check_vma=False,
    )
```

time: 394 us -> 176 us (0.45); the launches traced: 389 us -> 175 us
  waiting for transfers between devices: 129 us -> 0 us
  Pallas kernels: 0 us -> 95.3 us
  matrix products: 73.1 us -> 0 us
  other arithmetic: 52.9 us -> 2.56 us
  local copies, waits for them, and re-layouts: 42.5 us -> 6.04 us
  starting transfers between devices: 25.1 us -> 0 us
  blocking collectives: 51.9 us -> 70.7 us
  between operations: 14.3 us -> 0.76 us
    pallas_call x0 -> x2, Pallas kernels: none -> 95.3 us  [the longest x1 66.4 us: body(): pl.pallas_call(functools.partial(layer_kernel, n_seq, n_ep, tokens), out_...]
    all_to_all x6 -> x0, waiting for transfers between devices: 76.2 us -> none  [the longest x1 47.2 us: body(): lax.all_to_all(answer, ('seq', 'ep'), split_axis=0, concat_axis=0, tiled=...]
    dot_general x38 -> x0, matrix products: 73.1 us -> none  [the longest x17 34.3 us: advance(): jnp.einsum('qd,kd->qk', query_flat, block_k, preferred_element_type=jnp.f...]
    all_gather x0 -> x1, blocking collectives: none -> 70.7 us  [body(): everyone = lax.all_gather(dense, ('seq', 'ep'), axis=0, tiled=True)]
    all_to_all x1 -> x0, blocking collectives: 51.9 us -> none  [body(): lax.all_to_all(outgoing, ('seq', 'ep'), split_axis=0, concat_axis=0, tile...]
    reduce_scatter x1 -> x0, waiting for transfers between devices: 31.9 us -> none  [body(): lax.psum_scatter(jnp.dot(picked, full_weight, preferred_element_type=jnp....]
    all_to_all x6 -> x0, starting transfers between devices: 25 us -> none  [the longest x1 5.17 us: body(): lax.all_to_all(outgoing_kv[2], 'seq', split_axis=1, concat_axis=0, tiled=...]
    mul x35 -> x0, other arithmetic: 23.6 us -> none  [the longest x17 11.8 us: advance(): exp_scores * block_vs.astype(jnp.float32)[None, :]]
  transfers between devices with their start and end apart: 8 -> 0, of which waited for: 8 -> 0; matrix products, arithmetic and copies ran while one was open for 35% -> 0% of each run, Pallas kernels for 0% -> 0%
where the time goes in v1:
time: 176 us; the launch traced here: 175 us
  Pallas kernels  95.3 us (54%)
  blocking collectives  70.7 us (40%)
  local copies, waits for them, and re-layouts  6.04 us (3%)
  other arithmetic  2.56 us (1%)
    all_gather x1, blocking collectives, body(): everyone = lax.all_gather(dense, ('seq', 'ep'), axis=0, tiled=True)  70.7 us
    pallas_call x1, Pallas kernels, body(): pl.pallas_call(functools.partial(layer_kernel, n_seq, n_ep, tokens), out_...  66.4 us
    pallas_call x1, Pallas kernels, body(): pl.pallas_call(functools.partial(attention_kernel, n_seq, n_ep, copies, t...  29 us
    unnamed x10, local copies, waits for them, and re-layouts  3.59 us

profile of v1, /device:TPU:0, one launch (start us, length us, event | category | flops | bytes accessed | tf_op | source)
XLA Modules:
  0.0 175.4 jit_solution(6728893934287189431)
XLA Ops:
  0.7 0.8 reduce_sum.27
  1.5 0.8 broadcast_divide_fusion
  2.2 0.8 select_reduce_fusion.1
  3.0 70.7 %all_gather.3 = f32[256,16]{1,0:T(8,128)S(1)} all-gather(f32[8,16]{1,0:T(8,128)S(1)} %select_reduce_fusion.1), channel_id=1, replica_groups=mesh['grp'=1,'seq'=8,'ep'=4] {'seq','ep'}, dimensions={0}, use_global_device_ids=true | all-gather | bytes 16896 | tf_op jit(solution)/shard_map/all_gather | solution.py:539
  73.7 0.1 select_reduce_fusion
  73.8 0.1 reshape.29
  73.9 0.1 broadcast_in_dim.40
  74.0 0.8 broadcast_in_dim.41.mix_ref
  74.7 0.0 copy-start.1
  74.8 0.0 copy-start.2
  74.8 0.0 copy-start.3
  74.8 1.4 copy_bitcast_fusion
  76.2 0.1 pad_maximum_fusion.kv_ref
  76.2 0.0 copy-done.1
  76.3 0.1 copy.40
  76.3 0.0 copy-done.2
  76.4 0.0 copy-done.3
  76.4 29.0 %attention.1.attn_ref = bf16[64,1024]{1,0:T(8,128)(2,1)S(1)} custom-call(bf16[8,64,128]{2,1,0:T(8,128)(2,1)S(1)} %bitcast.18, bf16[4,1088,128]{2,1,0:T(8,128)(2,1)S(1)} %pad_maximum_fusion.kv_ref, f32[4,8,544]{2,1,0:T(8,128)S(1)} %fusion.3.scale_ref), custom_call_target="tpu_custom_call" | custom-call | tf_op jit(solution)/shard_map/attention/pallas_call | solution.py:559
  105.4 0.0 copy-start
  105.4 0.6 copy-done
  106.1 66.4 %layer.1 = (bf16[8,4096]{1,0:T(8,128)(2,1)}, bf16[8,4096]{1,0:T(8,128)(2,1)}) custom-call(bf16[64,1024]{1,0:T(8,128)(2,1)} %copy-done, bf16[1024,1024]{1,0:T(8,128)(2,1)} %out_weight_ref.1, bf16[8,4096]{1,0:T(8,128)(2,1)} %residual_ref.1, f32[1,4096]{1,0:T(1,128)} %bitcast.20, f32[256,128]{1,0:T(8,128)} %broadcast_in_dim.41.mix_ref, ...), custom_call_target="tpu_custom_call" | custom-call | tf_op jit(solution)/shard_map/layer/pallas_call | solution.py:592
  172.4 1.5 copy.43
  173.9 1.5 copy.44
  (5 shorter events, 0.1 us)
Async XLA Ops:
  74.7 1.5 copy-start.1
  74.8 1.6 copy-start.2
  74.8 1.6 copy-start.3
  105.4 0.6 copy-start

commit v2 on v1

--- a/solution.py
+++ b/solution.py
@@ -115,7 +115,7 @@
     for c in q_copies:
         c.wait_recv()
 
-    row_tile = 128
+    row_tile = 256
     row_tiles = n_seq * rows_each // row_tile
     inverse = 1.0 / math.sqrt(head_dim)
 
@@ -202,6 +202,9 @@
     hidden_ref,
     expert_ref,
     attn_all,
+    mix_line,
+    mix_all,
+    mix_rows,
     out_w,
     gate_w,
     up_w,
@@ -225,6 +228,10 @@
     tail_in,
     load_sem,
     local_sem,
+    line_send,
+    line_recv,
+    mix_send,
+    mix_recv,
     attn_send,
     attn_recv,
     part_send,
@@ -295,6 +302,19 @@
         )
         for j in range(1, n_ep)
     ]
+    line_keep = pltpu.make_async_copy(mix_ref, mix_line.at[zed], local_sem.at[3])
+    line_keep.start()
+    line_waits = [
+        go(
+            mix_ref,
+            mix_line.at[zed],
+            line_send.at[j],
+            line_recv.at[j],
+            me,
+            (zed + j) % n_ep,
+        )
+        for j in range(1, n_ep)
+    ]
     own.wait()
     loads[0].wait()
     for c in waits:
@@ -324,6 +344,22 @@
                 zed,
             )
         )
+    line_keep.wait()
+    for c in line_waits:
+        c.wait_recv()
+    mix_keep = pltpu.make_async_copy(mix_line, mix_all.at[me], local_sem.at[4])
+    mix_keep.start()
+    mix_waits = [
+        go(
+            mix_line,
+            mix_all.at[me],
+            mix_send.at[step],
+            mix_recv.at[step],
+            (me + step) % n_seq,
+            zed,
+        )
+        for step in range(1, n_seq)
+    ]
     for c in part_waits:
         c.wait_recv()
     summed = part_out[me].astype(f32)
@@ -373,6 +409,17 @@
         at = gathered.at[core, chip, (zed + n_ep - j) % n_ep]
         spread(at, at, j)
         across(at, at, 0, j)
+    mix_keep.wait()
+    for c in mix_waits:
+        c.wait_recv()
+    expert = (me * n_ep + zed) // 2
+    lane = lax.broadcasted_iota(jnp.int32, (1, mix_ref.shape[1]), 1)
+    group_rows = n_ep * tokens
+    for s in range(n_seq):
+        weights = mix_all[s].reshape(group_rows, mix_ref.shape[1])
+        weights = jnp.sum(jnp.where(lane == expert, weights, 0.0), axis=1, keepdims=True)
+        at = pl.ds(((s % 2) * chips + s // 2) * group_rows, group_rows)
+        mix_rows[at, :] = jnp.broadcast_to(weights, (group_rows, 128))
     for j in range(n_ep):
         for i in range(1, chips):
             b_waits[i, j].wait_recv()
@@ -432,7 +479,7 @@
             for n in range(width // 256):
                 deep = pl.ds(ch * width + n * 256, 256)
                 y = jnp.dot(active[at, :], down_w[:, deep], preferred_element_type=f32)
-                partial[ch, at, pl.ds(n * 256, 256)] = (y * mix_ref[at, :1]).astype(bf16)
+                partial[ch, at, pl.ds(n * 256, 256)] = (y * mix_rows[at, :1]).astype(bf16)
         theirs = pl.ds(pl.multiple_of((1 - core) * my_rows, 16), my_rows)
         pair_waits[ch] = go(
             partial.at[ch, theirs],
@@ -536,11 +583,8 @@
     dense = jnp.sum(
         jnp.where(route_ids[:, :, None] == grid[None, None, :], mix[:, :, None], 0.0), axis=1
     )
-    everyone = lax.all_gather(dense, ("seq", "ep"), axis=0, tiled=True)
-    expert = (lax.axis_index("seq") * n_ep + lax.axis_index("ep")) // 2
-    my_mix = jnp.sum(jnp.where(grid[None, :] == expert, everyone, 0.0), axis=1)
-    my_mix = my_mix.reshape(n_seq // 2, 2, n_ep * tokens).transpose(1, 0, 2)
-    my_mix = jnp.broadcast_to(my_mix.reshape(window_len, 1), (window_len, 128))
+    lanes = -(-experts // 128) * 128
+    dense = jnp.pad(dense, ((0, 0), (0, lanes - experts)))
 
     q_sorted = (
         queries.reshape(tokens, n_seq, heads, head_dim)
@@ -599,6 +643,9 @@
         out_specs=(vmem, vmem),
         scratch_shapes=[
             pltpu.VMEM((n_ep, n_seq * tokens, depth), bf16),
+            pltpu.VMEM((n_ep, tokens, lanes), f32),
+            pltpu.VMEM((n_seq, n_ep, tokens, lanes), f32),
+            pltpu.VMEM((window_len, 128), f32),
             pltpu.VMEM((depth, cols), bf16),
             pltpu.VMEM((model, wide), bf16),
             pltpu.VMEM((model, wide), bf16),
@@ -621,7 +668,11 @@
             pltpu.VMEM((chunks, n_ep, 2 * tokens, width // 2), bf16),
             pltpu.VMEM((chunks, n_ep, 2 * tokens, width // 2), bf16),
             dma((4,)),
-            dma((3,)),
+            dma((5,)),
+            dma((n_ep,)),
+            dma((n_ep,)),
+            dma((n_seq,)),
+            dma((n_seq,)),
             dma((n_ep,)),
             dma((n_ep,)),
             dma((n_seq,)),
@@ -650,7 +701,7 @@
         out_weight,
         residual,
         norm_gain.reshape(1, model),
-        my_mix,
+        dense,
         w_gate,
         w_up,
         w_down,

time: 176 us -> 106 us (0.60)
  blocking collectives: 70.7 us -> 0 us
  Pallas kernels: 95.3 us -> 98.6 us
  other arithmetic: 2.56 us -> 0.4 us
    all_gather x1 -> x0, blocking collectives: 70.7 us -> none  [body(): everyone = lax.all_gather(dense, ('seq', 'ep'), axis=0, tiled=True)]
    pallas_call x1, Pallas kernels: 66.4 us -> 71.1 us  [body(): pl.pallas_call(functools.partial(layer_kernel, n_seq, n_ep, tokens), out_...]
    unnamed x10 -> x14, local copies, waits for them, and re-layouts: 3.59 us -> 3.61 us
where the time goes in v2:
time: 106 us; the launch traced here: 105 us
  Pallas kernels  98.6 us (93%)
  local copies, waits for them, and re-layouts  5.75 us (5%)
    pallas_call x1, Pallas kernels, body(): pl.pallas_call(functools.partial(layer_kernel, n_seq, n_ep, tokens), out_...  71.1 us
    pallas_call x1, Pallas kernels, body(): pl.pallas_call(functools.partial(attention_kernel, n_seq, n_ep, copies, t...  27.4 us
    unnamed x14, local copies, waits for them, and re-layouts  3.61 us

profile of v2, /device:TPU:0, one launch (start us, length us, event | category | flops | bytes accessed | tf_op | source)
XLA Modules:
  0.0 105.5 jit_solution(904162162090704281)
XLA Ops:
  0.6 0.0 copy-start.1
  0.6 0.0 copy-start.3
  0.7 0.0 copy-start.4
  0.7 1.4 %copy_bitcast_fusion = (bf16[4,544,128]{2,1,0:T(8,128)(2,1)S(1)}, bf16[4,544,128]{2,1,0:T(8,128)(2,1)S(1)}) fusion(bf16[544,4,128]{2,1,0:T(4,128)(2,1)} %param.15, bf16[544,4,128]{2,1,0:T(4,128)(2,1)} %param.14), kind=kLoop, calls=%fused_computation.1 | loop fusion | bytes 2228224 | tf_op jit(solution)/shard_map/transpose | solution.py:595
  2.1 0.0 copy-start.2
  2.1 0.0 copy-start.5
  2.1 0.1 pad_maximum_fusion.kv_ref
  2.2 0.0 copy-done.1
  2.2 0.1 copy.31
  2.3 0.0 copy-done.3
  2.3 0.0 copy-done.4
  2.4 27.4 %attention.1.attn_ref = bf16[64,1024]{1,0:T(8,128)(2,1)S(1)} custom-call(bf16[8,64,128]{2,1,0:T(8,128)(2,1)S(1)} %bitcast.17, bf16[4,1088,128]{2,1,0:T(8,128)(2,1)S(1)} %pad_maximum_fusion.kv_ref, f32[4,8,544]{2,1,0:T(8,128)S(1)} %fusion.3.scale_ref), custom_call_target="tpu_custom_call" | custom-call | tf_op jit(solution)/shard_map/attention/pallas_call | solution.py:603
  29.8 0.0 copy-start
  29.8 0.6 copy-done
  30.5 0.0 copy-done.2
  30.5 0.1 reduce_sum.18
  30.6 0.1 broadcast_divide_fusion
  30.7 0.0 copy-done.5
  30.7 0.1 select_reduce_fusion
  30.8 0.6 pad.12.mix_ref
  31.4 71.1 %layer.1 = (bf16[8,4096]{1,0:T(8,128)(2,1)}, bf16[8,4096]{1,0:T(8,128)(2,1)}) custom-call(bf16[64,1024]{1,0:T(8,128)(2,1)} %copy-done, bf16[1024,1024]{1,0:T(8,128)(2,1)} %out_weight_ref.1, bf16[8,4096]{1,0:T(8,128)(2,1)} %residual_ref.1, f32[1,4096]{1,0:T(1,128)} %bitcast.19, f32[8,128]{1,0:T(8,128)} %pad.12.mix_ref, bf16[4096,384]{1,0:T(8,128)(2,1)} %gate_ref.1, ...), custom_call_target="tpu_custom_call" | custom-call | tf_op jit(solution)/shard_map/layer/pallas_call | solution.py:636
  102.5 1.5 %copy.34 = bf16[8,4096]{1,0:T(8,128)(2,1)} copy(bf16[8,4096]{1,0:T(8,128)(2,1)} %get-tuple-element.6) | data formatting | bytes 131072
  104.0 1.5 %copy.35 = bf16[8,4096]{1,0:T(8,128)(2,1)} copy(bf16[8,4096]{1,0:T(8,128)(2,1)} %get-tuple-element.7) | data formatting | bytes 131072
  (3 shorter events, 0.1 us)
Async XLA Ops:
  0.6 1.6 %copy-start.1 = (bf16[8,64,128]{2,1,0:T(8,128)(2,1)S(1)}, bf16[8,64,128]{2,1,0:T(8,128)(2,1)}, u32[]{:S(2)}) copy-start(bf16[8,64,128]{2,1,0:T(8,128)(2,1)} %param.13) | copy-start | bytes 393220
  0.6 1.7 %copy-start.3 = (bf16[544,4]{0,1:T(4,128)(2,1)S(1)}, bf16[544,4]{0,1:T(4,128)(2,1)}, u32[]{:S(2)}) copy-start(bf16[544,4]{0,1:T(4,128)(2,1)} %param.16) | copy-start | bytes 13060
  0.7 1.7 %copy-start.4 = (bf16[544,4]{0,1:T(4,128)(2,1)S(1)}, bf16[544,4]{0,1:T(4,128)(2,1)}, u32[]{:S(2)}) copy-start(bf16[544,4]{0,1:T(4,128)(2,1)} %param.17) | copy-start | bytes 13060
  2.1 28.4 %copy-start.2 = (f32[8,8]{1,0:T(8,128)S(1)}, f32[8,8]{1,0:T(8,128)}, u32[]{:S(2)}) copy-start(f32[8,8]{1,0:T(8,128)} %param.22) | copy-start | bytes 772
  2.1 28.6 %copy-start.5 = (s32[8,8]{1,0:T(8,128)S(1)}, s32[8,8]{1,0:T(8,128)}, u32[]{:S(2)}) copy-start(s32[8,8]{1,0:T(8,128)} %param.21) | copy-start | bytes 772
  29.8 0.6 copy-start

commit v3 on v2

--- a/solution.py
+++ b/solution.py
@@ -28,7 +28,8 @@
     )
 
 
-def attention_kernel(
+def attention_part(
+    go,
     n_seq,
     n_ep,
     copies,
@@ -38,7 +39,6 @@
     q_ref,
     kv_ref,
     scale_ref,
-    out_ref,
     q_all,
     kv_all,
     scale_all,
@@ -53,6 +53,9 @@
     scale_send,
     scale_recv,
     own_sem,
+    attn_all,
+    attn_send,
+    attn_recv,
 ):
     me = lax.axis_index("seq")
     zed = lax.axis_index("ep")
@@ -63,20 +66,12 @@
     local_len = scale_ref.shape[2]
     rows_each = tokens * heads
 
-    barrier = pltpu.get_barrier_semaphore()
-    for step in range(1, n_seq):
-        pl.semaphore_signal(
-            barrier,
-            inc=1,
-            device_id=device_at((me + step) % n_seq, zed),
-            device_id_type=MESH,
-        )
     own = pltpu.make_async_copy(q_ref.at[me], q_all.at[me], own_sem)
     own.start()
     top[...] = jnp.full_like(top, hidden_score)
     total[...] = jnp.zeros_like(total)
     acc[...] = jnp.zeros_like(acc)
-    pl.semaphore_wait(barrier, n_seq - 1)
+    pl.semaphore_wait(pltpu.get_barrier_semaphore(), n_seq + n_ep - 2)
 
     pending = []
     q_copies = []
@@ -119,7 +114,7 @@
     row_tiles = n_seq * rows_each // row_tile
     inverse = 1.0 / math.sqrt(head_dim)
 
-    def attend(kv, scales, i, q):
+    def attend(kv, scales, i, q, first=0, last=row_tiles):
         source = ((group + groups - i) % groups) * copies + (member + copies - q) % copies
 
         def one_tile(n, unused):
@@ -148,7 +143,7 @@
             top[at, :] = new
             return unused
 
-        lax.fori_loop(0, row_tiles, one_tile, 0)
+        lax.fori_loop(first, last, one_tile, 0)
 
     attend(kv_ref.at[group], scale_ref.at[group], 0, 0)
     for q in range(1, copies):
@@ -167,31 +162,52 @@
                 group * copies + (member + q) % copies,
             )
         attend(kv_all.at[i, 0], scale_all.at[i, 0], i, 0)
-    for i in range(1, groups):
-        for q in range(1, copies):
-            for c in arrivals[i, q]:
-                c.wait_recv()
-            attend(kv_all.at[i, q], scale_all.at[i, q], i, q)
-
-    for src in range(n_seq):
-        for h in range(heads):
-            at = pl.ds(src * rows_each + h * tokens, tokens)
-            wide[pl.ds(src * tokens, tokens), pl.ds(h * head_dim, head_dim)] = (
-                acc[at, :] / total[at, :]
+    tile_tokens = row_tile // heads
+    waits = []
+    for n in range(row_tiles):
+        for i in range(1, groups):
+            for q in range(1, copies):
+                if n == 0:
+                    for c in arrivals[i, q]:
+                        c.wait_recv()
+                attend(kv_all.at[i, q], scale_all.at[i, q], i, q, n, n + 1)
+        for src in range(n * tile_tokens // tokens, (n + 1) * tile_tokens // tokens):
+            for h in range(heads):
+                at = pl.ds(src * rows_each + h * tokens, tokens)
+                wide[pl.ds(src * tokens, tokens), pl.ds(h * head_dim, head_dim)] = (
+                    acc[at, :] / total[at, :]
+                )
+        at = pl.ds(n * tile_tokens, tile_tokens)
+        attn_all[zed, at, :] = wide[at, :].astype(jnp.bfloat16)
+        for j in range(1, n_ep):
+            waits.append(
+                go(
+                    attn_all.at[zed, at],
+                    attn_all.at[zed, at],
+                    attn_send.at[n, j],
+                    attn_recv.at[n, j],
+                    me,
+                    (zed + j) % n_ep,
+                )
             )
-    out_ref[...] = wide[...].astype(jnp.bfloat16)
     for c in q_copies:
         c.wait_send()
     for pair in pending:
         for c in pair:
             c.wait_send()
+    return waits
 
 
 def layer_kernel(
     n_seq,
     n_ep,
     tokens,
-    attn_ref,
+    copies,
+    heads,
+    prefix_len,
+    q_ref,
+    kv_ref,
+    scale_ref,
     out_weight_ref,
     residual_ref,
     gain_ref,
@@ -201,6 +217,20 @@
     down_ref,
     hidden_ref,
     expert_ref,
+    q_all,
+    kv_all,
+    scale_all,
+    top,
+    total,
+    acc,
+    tall,
+    q_send,
+    q_recv,
+    kv_send,
+    kv_recv,
+    scale_send,
+    scale_recv,
+    own_sem,
     attn_all,
     mix_line,
     mix_all,
@@ -221,9 +251,7 @@
     active,
     partial,
     pair_in,
-    pair_sum,
     plane_in,
-    tail_own,
     tail_out,
     tail_in,
     load_sem,
@@ -279,10 +307,6 @@
         pl.semaphore_signal(
             barrier, inc=1, device_id=device_at(me, (zed + step) % n_ep), device_id_type=MESH
         )
-    own = pltpu.make_async_copy(attn_ref, attn_all.at[zed], local_sem.at[0])
-    own.start()
-    pl.semaphore_wait(barrier, n_seq + n_ep - 2)
-
     sends = []
 
     def go(*args):
@@ -291,17 +315,35 @@
         sends.append(c)
         return c
 
-    waits = [
-        go(
-            attn_ref,
-            attn_all.at[zed],
-            attn_send.at[j],
-            attn_recv.at[j],
-            me,
-            (zed + j) % n_ep,
-        )
-        for j in range(1, n_ep)
-    ]
+    waits = attention_part(
+        go,
+        n_seq,
+        n_ep,
+        copies,
+        tokens,
+        heads,
+        prefix_len,
+        q_ref,
+        kv_ref,
+        scale_ref,
+        q_all,
+        kv_all,
+        scale_all,
+        top,
+        total,
+        acc,
+        tall,
+        q_send,
+        q_recv,
+        kv_send,
+        kv_recv,
+        scale_send,
+        scale_recv,
+        own_sem,
+        attn_all,
+        attn_send,
+        attn_recv,
+    )
     line_keep = pltpu.make_async_copy(mix_ref, mix_line.at[zed], local_sem.at[3])
     line_keep.start()
     line_waits = [
@@ -315,13 +357,12 @@
         )
         for j in range(1, n_ep)
     ]
-    own.wait()
     loads[0].wait()
     for c in waits:
         c.wait_recv()
 
     cols = out_w.shape[1]
-    depth = attn_ref.shape[1]
+    depth = attn_all.shape[2]
     part_waits = []
     attention = attn_all[...].reshape(n_ep * n_seq * tokens, depth)
     col_tile = 256
@@ -463,8 +504,14 @@
         return unused
 
     lax.fori_loop(0, model // depth_tile, contract, 0)
-    gate = gate_acc[...]
-    active[...] = (gate / (1.0 + jnp.exp(-gate)) * up_acc[...]).astype(bf16)
+
+    def activate(n, unused):
+        at = pl.ds(pl.multiple_of(n * 64, 64), 64)
+        gate = gate_acc[at, :]
+        active[at, :] = (gate / (1.0 + jnp.exp(-gate)) * up_acc[at, :]).astype(bf16)
+        return unused
+
+    lax.fori_loop(0, count // 64, activate, 0)
 
     chunks = partial.shape[0]
     width = partial.shape[2]
@@ -493,12 +540,12 @@
     def over_pair(ch):
         pair_waits[ch].wait_recv()
         ours = pl.ds(pl.multiple_of(core * my_rows, 16), my_rows)
-        pair_sum[ch] = (partial[ch, ours, :].astype(f32) + pair_in[ch].astype(f32)).astype(bf16)
+        pair_in[ch] = (partial[ch, ours, :].astype(f32) + pair_in[ch].astype(f32)).astype(bf16)
         for i in range(1, chips):
             goal = (chip + i) % chips
             plane_waits[ch, i] = go(
-                pair_sum.at[ch, pl.ds(pl.multiple_of(goal * chip_rows, 16), chip_rows)],
-                plane_in.at[ch, i],
+                pair_in.at[ch, pl.ds(pl.multiple_of(goal * chip_rows, 16), chip_rows)],
+                plane_in.at[ch, i - 1],
                 plane_send.at[ch, i],
                 plane_recv.at[ch, i],
                 goal * 2 + core,
@@ -509,10 +556,9 @@
         for i in range(1, chips):
             plane_waits[ch, i].wait_recv()
         ours = pl.ds(pl.multiple_of(chip * chip_rows, 16), chip_rows)
-        value = pair_sum[ch, ours, :].astype(f32)
+        value = pair_in[ch, ours, :].astype(f32)
         for i in range(1, chips):
-            value = value + plane_in[ch, i].astype(f32)
-        tail_own[ch] = value.reshape(n_ep, tokens, width)
+            value = value + plane_in[ch, i - 1].astype(f32)
         for j in range(n_ep):
             block = value[j * tokens : (j + 1) * tokens]
             tail_out[ch, j] = jnp.concatenate(
@@ -530,7 +576,8 @@
             )
 
     def finish(ch):
-        value = tail_own[ch, zed]
+        got = tail_out[ch, zed].astype(f32)
+        value = jnp.concatenate([got[:tokens], got[tokens:]], axis=1)
         for j in range(1, n_ep):
             tail_waits[ch, j].wait_recv()
             got = tail_in[ch, j].astype(f32)
@@ -600,11 +647,22 @@
     vmem = pl.BlockSpec(memory_space=pltpu.VMEM)
     hbm = pl.BlockSpec(memory_space=pl.ANY)
     dma = pltpu.SemaphoreType.DMA
-    attention = pl.pallas_call(
-        functools.partial(attention_kernel, n_seq, n_ep, copies, tokens, heads, prefix_len),
-        out_shape=jax.ShapeDtypeStruct((n_seq * tokens, heads * head_dim), bf16),
-        in_specs=[vmem] * 3,
-        out_specs=vmem,
+    cols = out_weight.shape[1]
+    depth = out_weight.shape[0]
+    wide = w_gate.shape[1]
+    chips = n_seq // 2
+    chunks = 2
+    width = model // chunks
+    return pl.pallas_call(
+        functools.partial(
+            layer_kernel, n_seq, n_ep, tokens, copies, heads, prefix_len
+        ),
+        out_shape=(
+            jax.ShapeDtypeStruct((tokens, model), bf16),
+            jax.ShapeDtypeStruct((tokens, model), bf16),
+        ),
+        in_specs=[vmem, vmem, vmem, hbm, vmem, vmem, vmem, hbm, hbm, hbm],
+        out_specs=(vmem, vmem),
         scratch_shapes=[
             pltpu.VMEM((n_seq, heads * tokens, head_dim), bf16),
             pltpu.VMEM((groups, copies, 2 * local_len, head_dim), bf16),
@@ -620,28 +678,6 @@
             dma((groups, copies)),
             dma((groups, copies)),
             dma,
-        ],
-        compiler_params=pltpu.CompilerParams(
-            collective_id=0, has_side_effects=True, vmem_limit_bytes=40 << 20
-        ),
-        name="attention",
-    )(q_sorted, kv, scales)
-
-    cols = out_weight.shape[1]
-    depth = out_weight.shape[0]
-    wide = w_gate.shape[1]
-    chips = n_seq // 2
-    chunks = 4
-    width = model // chunks
-    return pl.pallas_call(
-        functools.partial(layer_kernel, n_seq, n_ep, tokens),
-        out_shape=(
-            jax.ShapeDtypeStruct((tokens, model), bf16),
-            jax.ShapeDtypeStruct((tokens, model), bf16),
-        ),
-        in_specs=[vmem, hbm, vmem, vmem, vmem, hbm, hbm, hbm],
-        out_specs=(vmem, vmem),
-        scratch_shapes=[
             pltpu.VMEM((n_ep, n_seq * tokens, depth), bf16),
             pltpu.VMEM((n_ep, tokens, lanes), f32),
             pltpu.VMEM((n_seq, n_ep, tokens, lanes), f32),
@@ -662,9 +698,7 @@
             pltpu.VMEM((window_len, wide), bf16),
             pltpu.VMEM((chunks, window_len, width), bf16),
             pltpu.VMEM((chunks, window_len // 2, width), bf16),
-            pltpu.VMEM((chunks, window_len // 2, width), bf16),
-            pltpu.VMEM((chunks, chips, n_ep * tokens, width), bf16),
-            pltpu.VMEM((chunks, n_ep, tokens, width), f32),
+            pltpu.VMEM((chunks, chips - 1, n_ep * tokens, width), bf16),
             pltpu.VMEM((chunks, n_ep, 2 * tokens, width // 2), bf16),
             pltpu.VMEM((chunks, n_ep, 2 * tokens, width // 2), bf16),
             dma((4,)),
@@ -673,8 +707,8 @@
             dma((n_ep,)),
             dma((n_seq,)),
             dma((n_seq,)),
-            dma((n_ep,)),
-            dma((n_ep,)),
+            dma((q_rows // 256, n_ep)),
+            dma((q_rows // 256, n_ep)),
             dma((n_seq,)),
             dma((n_seq,)),
             dma((n_ep,)),
@@ -693,11 +727,13 @@
             dma((chunks, n_ep)),
         ],
         compiler_params=pltpu.CompilerParams(
-            collective_id=1, has_side_effects=True, vmem_limit_bytes=60 << 20
+            collective_id=0, has_side_effects=True, vmem_limit_bytes=63 << 20
         ),
         name="layer",
     )(
-        attention,
+        q_sorted,
+        kv,
+        scales,
         out_weight,
         residual,
         norm_gain.reshape(1, model),

time: 106 us -> 103 us (0.972)
  Pallas kernels: 98.6 us -> 93.9 us
  other arithmetic: 0.4 us -> 2.02 us
    pallas_call x2 -> x1, Pallas kernels: 98.6 us -> 93.9 us  [body(): pl.pallas_call(functools.partial(layer_kernel, n_seq, n_ep, tokens, copie...]
    unnamed x14 -> x12, local copies, waits for them, and re-layouts: 3.61 us -> 2.97 us
where the time goes in v3:
time: 103 us; the launch traced here: 102 us
  Pallas kernels  93.9 us (91%)
  local copies, waits for them, and re-layouts  5.76 us (6%)
  other arithmetic  2.02 us (2%)
    pallas_call x1, Pallas kernels, body(): pl.pallas_call(functools.partial(layer_kernel, n_seq, n_ep, tokens, copie...  93.9 us
    unnamed x12, local copies, waits for them, and re-layouts  2.97 us

profile of v3, /device:TPU:0, one launch (start us, length us, event | category | flops | bytes accessed | tf_op | source)
XLA Modules:
  0.0 102.4 jit_solution(3100767439360337072)
XLA Ops:
  0.6 0.0 copy-start
  0.6 0.0 copy-start.2
  0.7 0.0 copy-start.3
  0.7 0.0 copy-start.1
  0.7 0.0 copy-start.4
  0.7 1.4 %copy_bitcast_fusion = (bf16[4,544,128]{2,1,0:T(8,128)(2,1)S(1)}, bf16[4,544,128]{2,1,0:T(8,128)(2,1)S(1)}) fusion(bf16[544,4,128]{2,1,0:T(4,128)(2,1)} %param.15, bf16[544,4,128]{2,1,0:T(4,128)(2,1)} %param.14), kind=kLoop, calls=%fused_computation.1 | loop fusion | bytes 2228224 | tf_op jit(solution)/shard_map/transpose | solution.py:642
  2.1 1.1 %pad_maximum_fusion.kv_ref = bf16[4,1088,128]{2,1,0:T(8,128)(2,1)} fusion(bf16[4,544,128]{2,1,0:T(8,128)(2,1)S(1)} %get-tuple-element.2, bf16[4,544,128]{2,1,0:T(8,128)(2,1)S(1)} %get-tuple-element.3), kind=kLoop, calls=%fused_computation | loop fusion | flops 2228224 | bytes 2228224 | tf_op jit(solution)/shard_map/concatenate | solution.py:641
  3.2 0.0 copy-done
  3.2 0.7 copy.31
  3.9 0.0 copy-done.2
  3.9 0.0 copy-done.3
  4.0 0.7 fusion.3.scale_ref
  4.6 0.0 copy-done.1
  4.6 0.1 reduce_sum.18
  4.8 0.1 broadcast_divide_fusion
  4.8 0.0 copy-done.4
  4.8 0.1 select_reduce_fusion
  4.9 0.6 pad.12.mix_ref
  5.5 93.9 %layer.1 = (bf16[8,4096]{1,0:T(8,128)(2,1)}, bf16[8,4096]{1,0:T(8,128)(2,1)}) custom-call(bf16[8,64,128]{2,1,0:T(8,128)(2,1)} %bitcast.17, bf16[4,1088,128]{2,1,0:T(8,128)(2,1)} %pad_maximum_fusion.kv_ref, f32[4,8,544]{2,1,0:T(8,128)} %fusion.3.scale_ref, bf16[1024,1024]{1,0:T(8,128)(2,1)} %out_weight_ref.1, bf16[8,4096]{1,0:T(8,128)(2,1)} %residual_ref.1, ...), custom_call_target="tpu_custom_call" | custom-call | tf_op jit(solution)/shard_map/layer/pallas_call | solution.py:656
  99.4 1.5 %copy.34 = bf16[8,4096]{1,0:T(8,128)(2,1)} copy(bf16[8,4096]{1,0:T(8,128)(2,1)} %get-tuple-element.6) | data formatting | bytes 131072
  100.9 1.5 %copy.35 = bf16[8,4096]{1,0:T(8,128)(2,1)} copy(bf16[8,4096]{1,0:T(8,128)(2,1)} %get-tuple-element.7) | data formatting | bytes 131072
  (2 shorter events, 0.0 us)
Async XLA Ops:
  0.6 2.6 %copy-start = (bf16[8,64,128]{2,1,0:T(8,128)(2,1)S(1)}, bf16[8,64,128]{2,1,0:T(8,128)(2,1)}, u32[]{:S(2)}) copy-start(bf16[8,64,128]{2,1,0:T(8,128)(2,1)} %param.13) | copy-start | bytes 393220
  0.6 3.3 %copy-start.2 = (bf16[544,4]{0,1:T(4,128)(2,1)S(1)}, bf16[544,4]{0,1:T(4,128)(2,1)}, u32[]{:S(2)}) copy-start(bf16[544,4]{0,1:T(4,128)(2,1)} %param.16) | copy-start | bytes 13060
  0.7 3.3 %copy-start.3 = (bf16[544,4]{0,1:T(4,128)(2,1)S(1)}, bf16[544,4]{0,1:T(4,128)(2,1)}, u32[]{:S(2)}) copy-start(bf16[544,4]{0,1:T(4,128)(2,1)} %param.17) | copy-start | bytes 13060
  0.7 4.0 %copy-start.1 = (f32[8,8]{1,0:T(8,128)S(1)}, f32[8,8]{1,0:T(8,128)}, u32[]{:S(2)}) copy-start(f32[8,8]{1,0:T(8,128)} %param.22) | copy-start | bytes 772
  0.7 4.2 %copy-start.4 = (s32[8,8]{1,0:T(8,128)S(1)}, s32[8,8]{1,0:T(8,128)}, u32[]{:S(2)}) copy-start(s32[8,8]{1,0:T(8,128)} %param.21) | copy-start | bytes 772
